TPU v7x, 32 devices: a whole 2x2x4 slice. The times are simulated.
32 devices in a mesh: tm: 4 (over y, core), tile: 8 (over z, x).
Axes of the slice: x: 2, y: 2, z: 4, core: 2. Of those that a mesh axis runs over, the one named last changes fastest.
Arguments:
- inputs: bfloat16 [12, 32, 160, 256], P('tm', 'tile'), may hold values from -6 to 6
- grad_out: bfloat16 [12, 32, 160, 256], P('tm', 'tile'), may hold values from -6 to 6
- weight: bfloat16 [3, 3, 3, 256, 256], replicated, may hold values from -0.078125 to 0.078125
- lengths: int32 [8], P('tile'), may hold values from 1 to 4, 24 in all
Outputs:
- grad_in: bfloat16 [12, 32, 160, 256], P('tm', 'tile')
- grad_weight: float32 [3, 3, 3, 256, 256], P(None, None, None, 'tile')
Inputs may be any that keep to these rules, and one draw needn't show every extreme that they name: Each tile owns 1 to 4 rows, the lengths sum to 24, and some tile owns exactly 4.
All inputs are finite; a program needn't handle non-finite values. No bound on the sum of `lengths` on one device may be relied on, other than what follows from the above.
Results may differ from a plain program's by a relative error of at most 0.001.
Values may be sent and summed in bfloat16 or wider, within the bound.
A program may use at most 192 MiB of HBM per device.

v0:
```python
import jax
import jax.numpy as jnp
from jax import lax
from jax.sharding import PartitionSpec as P


def from_behind(block, axis, distance):
    devices = range(lax.axis_size(axis))
    route = [(i - distance, i) for i in devices if i - distance in devices]
    return lax.ppermute(block, axis, route)


def transpose_conv(sequence, weight, count_out, rows, width):
    total = None
    for kt in range(3):
        for kh in range(3):
            for kw in range(3):
                g_slice = sequence[
                    2 - kt : 2 - kt + count_out, 2 - kh : 2 - kh + rows, 2 - kw : 2 - kw + width
                ]
                term = jnp.einsum(
                    "fhwd,cd->fhwc", g_slice, weight[kt, kh, kw], preferred_element_type=jnp.float32
                )
                total = term if total is None else total + term
    return total


def body(inputs, grad_out, weight, lengths):
    frames, rows, width, chans = inputs.shape
    count = lengths[0]
    live = (jnp.arange(rows, dtype=jnp.int32) < count)[None, :, None, None]
    inputs = jnp.where(live, inputs, jnp.zeros_like(inputs))
    grad_out = jnp.where(live, grad_out, jnp.zeros_like(grad_out))
    last_x = lax.dynamic_slice_in_dim(inputs, count - 1, 1, 1)
    last_g = lax.dynamic_slice_in_dim(grad_out, count - 1, 1, 1)
    above = from_behind((last_x, last_g), "tile", 1)
    below = from_behind((inputs[:, :1], grad_out[:, :1]), "tile", -1)

    def extend(block, prev_row, next_row):
        blank = jnp.zeros_like(block[:, :1])
        tall = jnp.concatenate([prev_row, block, blank], axis=1)
        tall = lax.dynamic_update_slice_in_dim(tall, next_row, count + 1, 1)
        return jnp.pad(tall, ((0, 0), (0, 0), (1, 1), (0, 0)))

    x_wide = extend(inputs, above[0], below[0])
    g_wide = extend(grad_out, above[1], below[1])
    x_cache = from_behind(x_wide[frames - 2 :], "tm", 1)
    x_full = jnp.concatenate([x_cache, x_wide], axis=0)
    pieces = []
    for kt in range(3):
        for kh in range(3):
            for kw in range(3):
                x_slice = x_full[kt : kt + frames, kh : kh + rows, kw : kw + width]
                pieces.append(
                    jnp.einsum(
                        "fhwc,fhwd->cd", x_slice, grad_out, preferred_element_type=jnp.float32
                    )
                )
    local_weight = jnp.stack(pieces).reshape(3, 3, 3, chans, chans)
    g_next = from_behind(g_wide[:2], "tm", -1)
    grad_sum = transpose_conv(
        jnp.concatenate([g_wide, g_next], axis=0), weight, frames, rows, width
    )
    grad_in = jnp.where(live, grad_sum, jnp.zeros_like(grad_sum)).astype(jnp.bfloat16)
    shared = lax.psum_scatter(local_weight, "tile", scatter_dimension=3, tiled=True)
    grad_weight = lax.psum(shared, "tm")
    return (grad_in, grad_weight)


def solution(mesh):
    placed = (P("tm", "tile", None, None), P("tm", "tile", None, None), P(), P("tile"))
    return jax.shard_map(
        body,
        mesh=mesh,
        in_specs=placed,
        out_specs=(P("tm", "tile", None, None), P(None, None, None, "tile", None)),
        check_vma=False,
    )
```

profile of v0, /device:TPU:0, one launch (start us, length us, event | category | flops | bytes accessed | tf_op | source)
XLA Modules:
  0.0 245.2 jit_solution(17255375899727374264)
XLA Ops:
  10.3 4.8 %collective-permute-start = (bf16[3,1,160,256]{3,2,1,0:T(8,128)(2,1)S(1)}, bf16[3,1,160,256]{3,2,1,0:T(8,128)(2,1)S(1)}, u32[]{:S(2)}, u32[]{:S(2)}) collective-permute-start(bf16[3,1,160,256]{3,2,1,0:T(8,128)(2,1)S(1)} %get-tuple-element.5), channel_id=1, source_target_pairs={{0,1},{1,2},{2,3},{3,4},{4,5},{5,6},{6,7},{8,9},{9,10},{10,11},{11... | collective-permute-start | bytes 737288 | tf_op jit(solution)/shard_map/ppermute | solution.py:10
  15.9 4.1 %collective-permute-start.3 = (bf16[3,1,160,256]{3,2,1,0:T(8,128)(2,1)S(1)}, bf16[3,1,160,256]{3,2,1,0:T(8,128)(2,1)}, u32[]{:S(2)}, u32[]{:S(2)}) collective-permute-start(bf16[3,1,160,256]{3,2,1,0:T(8,128)(2,1)S(1)} %get-tuple-element.3), channel_id=1, source_target_pairs={{0,1},{1,2},{2,3},{3,4},{4,5},{5,6},{6,7},{8,9},{9,10},{10,11},{11... | collective-permute-start | bytes 737288 | tf_op jit(solution)/shard_map/ppermute | solution.py:10
  22.2 8.7 %collective-permute-done.3 = bf16[3,1,160,256]{3,2,1,0:T(8,128)(2,1)} collective-permute-done((bf16[3,1,160,256]{3,2,1,0:T(8,128)(2,1)S(1)}, bf16[3,1,160,256]{3,2,1,0:T(8,128)(2,1)}, u32[]{:S(2)}, u32[]{:S(2)}) %collective-permute-start.3) | collective-permute-done | bytes 245792 | tf_op jit(solution)/shard_map/ppermute | solution.py:10
  53.1 2.9 %copy-done = f32[27,256,256]{2,1,0:T(8,128)} copy-done((f32[27,256,256]{2,1,0:T(8,128)}, f32[27,256,256]{2,1,0:T(8,128)S(1)}, u32[]{:S(2)}) %copy-start) | copy-done | bytes 7077912
  58.2 7.3 %collective-permute-done.1 = bf16[3,1,160,256]{3,2,1,0:T(8,128)(2,1)S(1)} collective-permute-done((bf16[3,1,160,256]{3,2,1,0:T(8,128)(2,1)S(1)}, bf16[3,1,160,256]{3,2,1,0:T(8,128)(2,1)S(1)}, u32[]{:S(2)}, u32[]{:S(2)}) %collective-permute-start.1) | collective-permute-done | bytes 245792 | tf_op jit(solution)/shard_map/ppermute | solution.py:10
  70.3 1.7 fusion.129
  76.2 1.8 fusion.136
  78.0 1.8 fusion.140
  79.7 1.8 fusion.144
  81.7 1.7 fusion.101
  83.4 1.8 fusion.104
  86.9 1.8 fusion.110
  90.5 1.8 fusion.62
  92.3 1.8 fusion.65
  95.8 1.7 fusion.71
  99.3 1.8 fusion.77
  102.8 1.8 fusion.83
  104.6 1.8 fusion.86
  108.1 1.8 fusion.92
  109.9 1.8 fusion.95
  113.4 85.9 %reduce-scatter.2.cloned.1.call-done = f32[3,3,3,32,256]{4,3,2,1,0:T(8,128)} async-done(((f32[3,3,3,256,256]{4,3,2,1,0:T(8,128)}), f32[3,3,3,32,256]{4,3,2,1,0:T(8,128)}) %reduce-scatter.2.cloned.1.call-update) | async-done | bytes 884752 | tf_op jit(solution)/shard_map/reduce_scatter | solution.py:65
  199.4 17.8 %select_convert_fusion = bf16[3,4,160,256]{3,2,1,0:T(8,128)(2,1)} fusion(f32[3,4,160,256]{3,2,1,0:T(8,128)} %fusion.136, f32[3,4,160,256]{3,2,1,0:T(8,128)S(1)} %fusion.125, f32[3,4,160,256]{3,2,1,0:T(8,128)} %fusion.127, f32[3,4,160,256]{3,2,1,0:T(8,128)} %fusion.140, f32[3,4,160,256]{3,2,1,0:T(8,128)} %fusion.129, f32[3,4,160,256]{3,2,1,0:T(8,128)} %fusion.131, ...), kind=kOutput, calls=%fused_computation.68 | convolution fusion | flops 265420800 | bytes 53706756 | tf_op jit(solution)/shard_map/fhwd,cd->fhwc/dot_general | solution.py:21
  217.1 19.0 %all-reduce.4.cloned.1.call-done = f32[3,3,3,32,256]{4,3,2,1,0:T(8,128)} async-done(((f32[3,3,3,32,256]{4,3,2,1,0:T(8,128)}), f32[3,3,3,32,256]{4,3,2,1,0:T(8,128)}) %all-reduce.4.cloned.1.call-update) | async-done | bytes 884752 | tf_op jit(solution)/shard_map/psum | solution.py:66
  236.1 2.2 copy.94
  (73 shorter events, 50.6 us)
Async XLA Ops:
  7.2 192.2 %reduce-scatter.2.cloned.1.call-start = ((), (), s32[]{:S(2)}) async-start(), calls=%async_computation.1 | async-start | bytes 7962624 | tf_op jit(solution)/shard_map/reduce_scatter | solution.py:65
  10.3 11.2 %collective-permute-start = (bf16[3,1,160,256]{3,2,1,0:T(8,128)(2,1)S(1)}, bf16[3,1,160,256]{3,2,1,0:T(8,128)(2,1)S(1)}, u32[]{:S(2)}, u32[]{:S(2)}) collective-permute-start(bf16[3,1,160,256]{3,2,1,0:T(8,128)(2,1)S(1)} %get-tuple-element.5), channel_id=1, source_target_pairs={{0,1},{1,2},{2,3},{3,4},{4,5},{5,6},{6,7},{8,9},{9,10},{10,11},{11... | collective-permute-start | bytes 737288 | tf_op jit(solution)/shard_map/ppermute | solution.py:10
  15.9 15.0 %collective-permute-start.3 = (bf16[3,1,160,256]{3,2,1,0:T(8,128)(2,1)S(1)}, bf16[3,1,160,256]{3,2,1,0:T(8,128)(2,1)}, u32[]{:S(2)}, u32[]{:S(2)}) collective-permute-start(bf16[3,1,160,256]{3,2,1,0:T(8,128)(2,1)S(1)} %get-tuple-element.3), channel_id=1, source_target_pairs={{0,1},{1,2},{2,3},{3,4},{4,5},{5,6},{6,7},{8,9},{9,10},{10,11},{11... | collective-permute-start | bytes 737288 | tf_op jit(solution)/shard_map/ppermute | solution.py:10
  20.0 12.2 %collective-permute-start.4 = (bf16[3,1,160,256]{3,2,1,0:T(8,128)(2,1)}, bf16[3,1,160,256]{3,2,1,0:T(8,128)(2,1)}, u32[]{:S(2)}, u32[]{:S(2)}) collective-permute-start(bf16[3,1,160,256]{3,2,1,0:T(8,128)(2,1)} %get-tuple-element.2), channel_id=1, source_target_pairs={{1,0},{2,1},{3,2},{4,3},{5,4},{6,5},{7,6},{9,8},{10,9},{11,10},{12... | collective-permute-start | bytes 737288 | tf_op jit(solution)/shard_map/ppermute | solution.py:10
  21.5 0.7 copy-start.3
  34.3 3.5 %collective-permute-start.5 = (bf16[2,6,162,256]{3,0,2,1:T(2,128)(2,1)S(1)}, bf16[2,6,162,256]{3,0,2,1:T(2,128)(2,1)S(1)}, u32[]{:S(2)}, u32[]{:S(2)}) collective-permute-start(bf16[2,6,162,256]{3,0,2,1:T(2,128)(2,1)S(1)} %copy.8), channel_id=1, source_target_pairs={{0,8},{8,16},{16,24},{1,9},{9,17},{17,25},{2,10},{10,18},{18,26},{... | collective-permute-start | bytes 2985992 | tf_op jit(solution)/shard_map/ppermute | solution.py:10
  53.1 2.9 %copy-start = (f32[27,256,256]{2,1,0:T(8,128)}, f32[27,256,256]{2,1,0:T(8,128)S(1)}, u32[]{:S(2)}) copy-start(f32[27,256,256]{2,1,0:T(8,128)S(1)} %fusion.3) | copy-start | bytes 21233668
  56.0 0.9 copy-start.2
  56.0 180.1 %all-reduce.4.cloned.1.call-start = ((), (), s32[]{:S(2)}) async-start(), calls=%async_computation.2 | async-start | bytes 1769472 | tf_op jit(solution)/shard_map/psum | solution.py:66
  56.9 8.6 %collective-permute-start.1 = (bf16[3,1,160,256]{3,2,1,0:T(8,128)(2,1)S(1)}, bf16[3,1,160,256]{3,2,1,0:T(8,128)(2,1)S(1)}, u32[]{:S(2)}, u32[]{:S(2)}) collective-permute-start(bf16[3,1,160,256]{3,2,1,0:T(8,128)(2,1)S(1)} %copy-done.2), channel_id=1, source_target_pairs={{1,0},{2,1},{3,2},{4,3},{5,4},{6,5},{7,6},{9,8},{10,9},{11,10},{12... | collective-permute-start | bytes 737288 | tf_op jit(solution)/shard_map/ppermute | solution.py:10
  65.6 2.5 %copy-start.1 = (bf16[3,3,3,256,256]{4,3,2,1,0:T(8,128)(2,1)S(1)}, bf16[3,3,3,256,256]{4,3,2,1,0:T(8,128)(2,1)}, u32[]{:S(2)}) copy-start(bf16[3,3,3,256,256]{4,3,2,1,0:T(8,128)(2,1)} %param.6) | copy-start | bytes 10616836
  66.6 14.9 %collective-permute-start.2 = (bf16[2,6,162,256]{3,0,2,1:T(2,128)(2,1)S(1)}, bf16[2,6,162,256]{3,0,2,1:T(2,128)(2,1)S(1)}, u32[]{:S(2)}, u32[]{:S(2)}) collective-permute-start(bf16[2,6,162,256]{3,0,2,1:T(2,128)(2,1)S(1)} %copy.6), channel_id=1, source_target_pairs={{8,0},{16,8},{24,16},{9,1},{17,9},{25,17},{10,2},{18,10},{26,18},{... | collective-permute-start | bytes 2985992 | tf_op jit(solution)/shard_map/ppermute | solution.py:10
Sparse Core Ops, SparseCore 0:
  56.1 143.1 reduce-scatter.1
  201.8 34.2 all-reduce.3
where the time goes:
time: 245 us
  waiting for transfers between devices  122 us (50%)
  matrix products  77.2 us (32%)
  between operations  15.1 us (6%)
  starting transfers between devices  14.6 us (6%)
  local copies, waits for them, and re-layouts  12.9 us (5%)
  other arithmetic  3.07 us (1%)
    reduce_scatter x1, waiting for transfers between devices, body(): lax.psum_scatter(local_weight, 'tile', scatter_dimension=3, tiled=True)  85.9 us
    dot_general x27, matrix products, transpose_conv(): jnp.einsum('fhwd,cd->fhwc', g_slice, weight[kt, kh, kw], preferred_elemen...  62.2 us
    psum x1, waiting for transfers between devices, body(): grad_weight = lax.psum(shared, 'tm')  19 us
    ppermute x6, waiting for transfers between devices, from_behind(): return lax.ppermute(block, axis, route)  17.4 us
    dot_general x27, matrix products, body(): jnp.einsum('fhwc,fhwd->cd', x_slice, grad_out, preferred_element_type=jnp...  15 us
    ppermute x6, starting transfers between devices, from_behind(): return lax.ppermute(block, axis, route)  14.5 us
    unnamed x9, local copies, waits for them, and re-layouts  6.63 us
  transfers between devices with their start and end apart: 8, of which 6 were waited for; matrix products, arithmetic and copies ran while one was open for 27% of the time, Pallas kernels for 0%

commit v1 on v0

v1 whole, which is shorter than its diff:
```python
import functools
import math

import jax
import jax.numpy as jnp
from jax import lax
from jax.experimental import pallas as pl
from jax.experimental.pallas import tpu as pltpu
from jax.sharding import PartitionSpec as P

F32, BF16, I16 = jnp.float32, jnp.bfloat16, jnp.int16
MESH = pl.DeviceIdType.MESH
LANES = 128
GROUPS = 9


def up16(n):
    return -(-n // 16) * 16


def encode(value):
    value = value.reshape(-1, LANES)
    rows = value.shape[0]
    most = jnp.max(jnp.abs(value), axis=0, keepdims=True)
    power = jnp.floor(jnp.log2(jnp.maximum(most, 1e-30))) + 1.0
    parts = [jnp.round(value * (jnp.exp2(-power) * 32000.0))]
    if rows % 16:
        parts.append(jnp.zeros((up16(rows) - rows, LANES), F32))
    parts.append(jnp.broadcast_to(power, (16, LANES)))
    return jnp.concatenate(parts, axis=0).astype(jnp.int32).astype(I16)


def decode(code, shape):
    rows = math.prod(shape) // LANES
    value = code.astype(jnp.int32).astype(F32)
    scale = jnp.exp2(value[-16:-15]) * (1.0 / 32000.0)
    return (value[:rows] * scale).reshape(shape)


def kernel(
    sizes, count_ref, x_ref, g_ref, w_hbm, dx_ref, dw_ref,
    w_ref, own, prev, nxt, last, shifted, patches, x_t, dx_acc, acc, part, done,
    a_out, a_in, x_out, x_in, z_out, z_in, fin,
    w_sem, row_send, row_recv, frame_send, frame_recv, rim_send, rim_recv,
    a_send, a_recv, x_send, x_recv, z_send, z_recv, f_send, f_recv,
):
    n_tm, n_tile, nx, nz, slab, frames, rows, width, chans = sizes
    tm, tile = lax.axis_index("tm"), lax.axis_index("tile")
    core, zi, xi = lax.rem(tm, 2), tile // nx, lax.rem(tile, nx)
    pair = tm + 1 - 2 * core
    behind = lax.rem(tm + n_tm - 1, n_tm)
    plane = rows * width
    count = count_ref[0]

    def copy(src, dst, send, recv, to_tm, to_tile):
        return pltpu.make_async_remote_copy(
            src_ref=src, dst_ref=dst, send_sem=send, recv_sem=recv,
            device_id=(to_tm, to_tile), device_id_type=MESH,
        )

    x_peers = [lax.rem(xi + k, nx) for k in range(1, nx)]
    z_peers = [lax.rem(zi + k, nz) for k in range(1, nz)]
    t_peers = [lax.rem(tm + k, n_tm) for k in range(1, n_tm)]

    load_w = pltpu.make_async_copy(w_hbm, w_ref, w_sem)
    load_w.start()

    barrier = pltpu.get_barrier_semaphore()
    greet = [(tm, lax.rem(tile + 1, n_tile)), (tm, lax.rem(tile + n_tile - 1, n_tile))]
    greet += [(tm, zi * nx + p) for p in x_peers]
    greet += [(tm, p * nx + xi) for p in z_peers]
    greet += [(p, tile) for p in t_peers]
    for who in greet:
        pl.semaphore_signal(barrier, inc=1, device_id=who, device_id_type=MESH)

    last[...] = g_ref[:, pl.ds(lax.rem(count + rows - 1, rows), 1)].reshape(frames, width, chans)
    pl.semaphore_wait(barrier, len(greet))

    first = g_ref.at[:, 0]
    down = copy(last, prev.at[pl.ds(0, frames)], row_send.at[0], row_recv.at[0], tm, lax.rem(tile + 1, n_tile))
    lift = copy(first, nxt.at[pl.ds(0, frames)], row_send.at[1], row_recv.at[1], tm, lax.rem(tile + n_tile - 1, n_tile))
    back = copy(g_ref.at[pl.ds(0, 2)], own, frame_send, frame_recv, behind, tile)
    rims = [
        copy(ref.at[pl.ds(0, 2)], ref.at[pl.ds(frames, 2)], rim_send.at[i], rim_recv.at[i], behind, tile)
        for i, ref in enumerate((prev, nxt))
    ]

    @pl.when(tile < n_tile - 1)
    def _():
        down.start()

    @pl.when(tile > 0)
    def _():
        lift.start()

    @pl.when(tm > 0)
    def _():
        back.start()

    @pl.when(tile == 0)
    def _():
        prev[pl.ds(0, frames)] = jnp.zeros((frames, width, chans), BF16)

    @pl.when(tile == n_tile - 1)
    def _():
        nxt[pl.ds(0, frames)] = jnp.zeros((frames, width, chans), BF16)

    @pl.when(tm == n_tm - 1)
    def _():
        own[...] = jnp.zeros((2, rows, width, chans), BF16)
        prev[pl.ds(frames, 2)] = jnp.zeros((2, width, chans), BF16)
        nxt[pl.ds(frames, 2)] = jnp.zeros((2, width, chans), BF16)

    def spread(row):
        wide = row.astype(F32)
        at = lax.broadcasted_iota(jnp.int32, (width, chans), 0)
        right = jnp.where(at == width - 1, 0.0, pltpu.roll(wide, width - 1, 0)).astype(BF16)
        left = jnp.where(at == 0, 0.0, pltpu.roll(wide, 1, 0)).astype(BF16)
        return jnp.concatenate([right, row, left], axis=-1)

    def center(frame, row, block):
        patches[1, frame, row] = spread(block)

    def rim(frame):
        top = spread(prev[frame])
        shifted[...] = spread(nxt[frame])
        patches[2, frame, 0] = top
        for r in range(1, rows):
            patches[2, frame, r] = patches[1, frame, r - 1]
        for r in range(rows - 1):
            inside = (r + 1 < count).astype(jnp.int32)
            keep = jnp.broadcast_to(inside, (width, 3 * chans)) > 0
            patches[0, frame, r] = jnp.where(
                keep, patches[1, frame, r + 1].astype(F32), shifted[...].astype(F32)
            ).astype(BF16)
        patches[0, frame, rows - 1] = shifted[...]

    def frame_inside(f, _):
        for r in range(rows):
            center(f, r, g_ref[f, r])
        masked = [
            x_ref[f, r].astype(F32) * (r < count).astype(F32) for r in range(rows)
        ]
        x_t[f] = jnp.concatenate(masked, axis=0).T.astype(BF16)
        return 0

    lax.fori_loop(0, frames, frame_inside, 0)

    def rows_arrive():
        @pl.when(tile > 0)
        def _():
            down.wait_recv()

        @pl.when(tile < n_tile - 1)
        def _():
            lift.wait_recv()

        @pl.when(tm > 0)
        def _():
            for r in rims:
                r.start()

        lax.fori_loop(0, frames, lambda f, _: (rim(f), 0)[1], 0)

    def frames_arrive():
        @pl.when(tm < n_tm - 1)
        def _():
            back.wait_recv()
            for r in rims:
                r.wait_recv()

        def one(f, _):
            for r in range(rows):
                center(frames + f, r, own[f, r])
            rim(frames + f)
            return 0

        lax.fori_loop(0, 2, one, 0)

    def taps(g):
        shift, j = g // 3, lax.rem(g, 3)
        return shift, lax.rem(j + 1, 3)

    def grad_w(g):
        shift, kh = taps(g)
        for k in range(3):
            total = None
            for f in range(frames):
                block = patches[kh, shift + f, :, :, k * chans : (k + 1) * chans]
                term = jnp.dot(x_t[f], block.reshape(plane, chans), preferred_element_type=F32)
                total = term if total is None else total + term
            for half in range(2):
                acc[g, 2 * k + half] = total[:, half * LANES : (half + 1) * LANES].reshape(
                    nz, nx, slab, LANES
                )
        a_out[g] = encode(acc[g, pl.ds(3 * (1 - core), 3)])
        send_a(g).start()

    def grad_x(g):
        shift, kh = taps(g)
        kernel_taps = [w_ref[2 - shift, kh, k] for k in range(3)]
        wide = jnp.concatenate(kernel_taps, axis=-1)
        for f in range(frames):
            block = patches[kh, shift + f].reshape(plane, 3 * chans)
            term = lax.dot_general(
                block, wide, (((1,), (1,)), ((), ())), preferred_element_type=F32
            )

            @pl.when(g == 0)
            def _():
                dx_acc[f] = term

            @pl.when(g > 0)
            def _():
                dx_acc[f] = dx_acc[f] + term

    def send_a(g):
        return copy(a_out.at[g], a_in.at[g], a_send.at[g], a_recv.at[g], pair, tile)

    def send_x(g, k):
        return copy(
            x_out.at[g, k], x_in.at[g, k], x_send.at[g, k], x_recv.at[g, k], tm, zi * nx + x_peers[k]
        )

    def send_z(g, k):
        return copy(
            z_out.at[g, k], z_in.at[g, k], z_send.at[g, k], z_recv.at[g, k], tm, z_peers[k] * nx + xi
        )

    def send_f(g, k):
        return copy(
            fin.at[g, tm], fin.at[g, tm], f_send.at[g, k], f_recv.at[g, n_tm - 2 - k], t_peers[k], tile
        )

    def pairs_step(g):
        send_a(g).wait_recv()
        mine = pl.ds(3 * core, 3)
        acc[g, mine] = acc[g, mine] + decode(a_in[g], (3, nz, nx, slab, LANES))
        for k in range(nx - 1):
            x_out[g, k] = encode(acc[g, mine, :, x_peers[k]])
            send_x(g, k).start()

    def x_step(g):
        total = acc[g, pl.ds(3 * core, 3), :, xi]
        for k in range(nx - 1):
            send_x(g, k).wait_recv()
            total = total + decode(x_in[g, k], (3, nz, slab, LANES))
        part[...] = total
        for k in range(nz - 1):
            z_out[g, k] = encode(part[:, z_peers[k]])
            send_z(g, k).start()
        done[g] = part[:, zi]

    def z_step(g):
        total = done[g]
        for k in range(nz - 1):
            send_z(g, k).wait_recv()
            total = total + decode(z_in[g, k], (3, slab, LANES))
        fin[g, tm] = encode(total)
        for k in range(n_tm - 1):
            send_f(g, k).start()

    def final_step(g):
        shift, kh = taps(g)
        for k in range(n_tm - 1):
            pltpu.make_async_remote_copy(
                src_ref=fin.at[g, tm], dst_ref=fin.at[g, t_peers[k]],
                send_sem=f_send.at[g, k], recv_sem=f_recv.at[g, k],
                device_id=(t_peers[k], tile), device_id_type=MESH,
            ).wait_recv()
        for half in range(2):
            total = None
            for y in range(n_tm // 2):
                term = decode(fin[g, 2 * y + half], (3, slab, LANES))
                total = term if total is None else total + term
            for j in range(3):
                lane = 3 * half + j
                at = (lane % 2) * LANES
                dw_ref[2 - shift, kh, lane // 2, :, at : at + LANES] = total[j]

    def step(s, _):
        @pl.when(s == 1)
        def _():
            rows_arrive()

        @pl.when(s == 3)
        def _():
            frames_arrive()

        @pl.when(s < GROUPS)
        def _():
            grad_w(s)

        @pl.when(s == GROUPS)
        def _():
            load_w.wait()

        @pl.when((s >= GROUPS) & (s < 2 * GROUPS))
        def _():
            grad_x(s - GROUPS)

        @pl.when((s >= 1) & (s < 1 + GROUPS))
        def _():
            pairs_step(s - 1)

        for start, act in ((8, final_step), (6, z_step), (4, x_step)):
            @pl.when((s >= start) & (s < start + 2 * GROUPS) & (lax.rem(s, 2) == 0))
            def _():
                act((s - start) // 2)

        return 0

    lax.fori_loop(0, 8 + 2 * GROUPS - 1, step, 0)

    for f in range(frames):
        for r in range(rows):
            used = (r < count).astype(F32)
            dx_ref[f, r] = (dx_acc[f, r * width : (r + 1) * width] * used).astype(BF16)

    @pl.when(tile < n_tile - 1)
    def _():
        down.wait_send()

    @pl.when(tile > 0)
    def _():
        lift.wait_send()

    @pl.when(tm > 0)
    def _():
        back.wait_send()
        for r in rims:
            r.wait_send()

    def drain(g, _):
        send_a(g).wait_send()
        for k in range(nx - 1):
            send_x(g, k).wait_send()
        for k in range(nz - 1):
            send_z(g, k).wait_send()
        for k in range(n_tm - 1):
            send_f(g, k).wait_send()
        return 0

    lax.fori_loop(0, GROUPS, drain, 0)


def body(inputs, grad_out, weight, lengths):
    frames, rows, width, chans = inputs.shape
    n_tm, n_tile = lax.axis_size("tm"), lax.axis_size("tile")
    nx = 2 ** (int(math.log2(n_tile)) // 2)
    nz = n_tile // nx
    slab = chans // n_tile
    sizes = (n_tm, n_tile, nx, nz, slab, frames, rows, width, chans)
    full = frames + 2
    a_rows = 3 * chans + 16
    x_rows = up16(3 * nz * slab) + 16
    z_rows = up16(3 * slab) + 16
    vmem, dma = pltpu.VMEM, pltpu.SemaphoreType.DMA
    flops = 4 * 27 * frames * rows * width * chans * chans
    dx, dw = pl.pallas_call(
        functools.partial(kernel, sizes),
        out_shape=(
            jax.ShapeDtypeStruct((frames, rows, width, chans), BF16),
            jax.ShapeDtypeStruct((3, 3, 3, slab, chans), F32),
        ),
        in_specs=[
            pl.BlockSpec(memory_space=pltpu.SMEM),
            pl.BlockSpec(memory_space=vmem),
            pl.BlockSpec(memory_space=vmem),
            pl.BlockSpec(memory_space=pl.ANY),
        ],
        out_specs=(pl.BlockSpec(memory_space=vmem), pl.BlockSpec(memory_space=vmem)),
        scratch_shapes=[
            vmem((3, 3, 3, chans, chans), BF16),
            vmem((2, rows, width, chans), BF16),
            vmem((full, width, chans), BF16),
            vmem((full, width, chans), BF16),
            vmem((frames, width, chans), BF16),
            vmem((width, 3 * chans), BF16),
            vmem((3, full, rows, width, 3 * chans), BF16),
            vmem((frames, chans, rows * width), BF16),
            vmem((frames, rows * width, chans), F32),
            vmem((GROUPS, 6, nz, nx, slab, LANES), F32),
            vmem((3, nz, slab, LANES), F32),
            vmem((GROUPS, 3, slab, LANES), F32),
            vmem((GROUPS, a_rows, LANES), I16),
            vmem((GROUPS, a_rows, LANES), I16),
            vmem((GROUPS, nx - 1, x_rows, LANES), I16),
            vmem((GROUPS, nx - 1, x_rows, LANES), I16),
            vmem((GROUPS, nz - 1, z_rows, LANES), I16),
            vmem((GROUPS, nz - 1, z_rows, LANES), I16),
            vmem((GROUPS, n_tm, z_rows, LANES), I16),
            dma, dma((2,)), dma((2,)), dma, dma, dma((2,)), dma((2,)),
            dma((GROUPS,)), dma((GROUPS,)),
            dma((GROUPS, nx - 1)), dma((GROUPS, nx - 1)),
            dma((GROUPS, nz - 1)), dma((GROUPS, nz - 1)),
            dma((GROUPS, n_tm - 1)), dma((GROUPS, n_tm - 1)),
        ],
        compiler_params=pltpu.CompilerParams(
            collective_id=0, has_side_effects=True, vmem_limit_bytes=60 * 2**20
        ),
        cost_estimate=pl.CostEstimate(flops=flops, bytes_accessed=8 * 2**20, transcendentals=0),
    )(lengths, inputs, grad_out, weight)
    return dx, dw


def solution(mesh):
    placed = (P("tm", "tile", None, None), P("tm", "tile", None, None), P(), P("tile"))
    return jax.shard_map(
        body,
        mesh=mesh,
        in_specs=placed,
        out_specs=(P("tm", "tile", None, None), P(None, None, None, "tile", None)),
        check_vma=False,
    )
```

time: 245 us -> 79.8 us (0.33)
  waiting for transfers between devices: 122 us -> 0 us
  matrix products: 77.2 us -> 0 us
  Pallas kernels: 0 us -> 73.9 us
  starting transfers between devices: 14.6 us -> 0 us
  between operations: 15.1 us -> 1.29 us
  local copies, waits for them, and re-layouts: 12.9 us -> 4.38 us
  other arithmetic: 3.07 us -> 0 us
    reduce_scatter x1 -> x0, waiting for transfers between devices: 85.9 us -> none  [body(): lax.psum_scatter(local_weight, 'tile', scatter_dimension=3, tiled=True)]
    dot_general x54 -> x0, matrix products: 77.2 us -> none  [the longest x27 62.2 us: transpose_conv(): jnp.einsum('fhwd,cd->fhwc', g_slice, weight[kt, kh, kw], preferred_elemen...]
    pallas_call x0 -> x1, Pallas kernels: none -> 73.9 us  [body(): pl.pallas_call(functools.partial(kernel, sizes), out_shape=(jax.ShapeDtyp...]
    psum x1 -> x0, waiting for transfers between devices: 19 us -> none  [body(): grad_weight = lax.psum(shared, 'tm')]
    ppermute x6 -> x0, waiting for transfers between devices: 17.4 us -> none  [from_behind(): return lax.ppermute(block, axis, route)]
    ppermute x6 -> x0, starting transfers between devices: 14.5 us -> none  [from_behind(): return lax.ppermute(block, axis, route)]
    slice x6 -> x0, local copies, waits for them, and re-layouts: 3.5 us -> none  [the longest x2 1.46 us: body(): below = from_behind((inputs[:, :1], grad_out[:, :1]), 'tile', -1)]
    unnamed x9 -> x2, local copies, waits for them, and re-layouts: 6.63 us -> 4.38 us
  transfers between devices with their start and end apart: 8 -> 0, of which waited for: 6 -> 0; matrix products, arithmetic and copies ran while one was open for 27% -> 0% of each run, Pallas kernels for 0% -> 0%
where the time goes in v1:
time: 79.8 us; the launch traced here: 79.5 us
  Pallas kernels  73.9 us (93%)
  local copies, waits for them, and re-layouts  4.38 us (5%)
  between operations  1.29 us (2%)
    pallas_call x1, Pallas kernels, body(): pl.pallas_call(functools.partial(kernel, sizes), out_shape=(jax.ShapeDtyp...  73.9 us
    unnamed x2, local copies, waits for them, and re-layouts  4.38 us

profile of v1, /device:TPU:0, one launch (start us, length us, event | category | flops | bytes accessed | tf_op | source)
XLA Modules:
  0.0 79.5 jit_solution(11615540581836325024)
XLA Ops:
  1.3 73.9 %shard_map.59 = (bf16[3,4,160,256]{3,2,1,0:T(8,128)(2,1)}, f32[3,3,3,32,256]{4,3,2,1,0:T(8,128)}) custom-call(s32[1]{0:T(128)S(6)} %copy.8.count_ref, bf16[3,4,160,256]{3,2,1,0:T(8,128)(2,1)} %x_ref.1, bf16[3,4,160,256]{3,2,1,0:T(8,128)(2,1)} %g_ref.1, bf16[3,3,3,256,256]{4,3,2,1,0:T(8,128)(2,1)} %w_hbm.1), custom_call_target="tpu_custom_call" | custom-call | flops 13589544960 | bytes 8388608 | tf_op jit(solution)/shard_map/pallas_call | solution.py:360
  75.1 2.2 %copy.9 = bf16[3,4,160,256]{3,2,1,0:T(8,128)(2,1)} copy(bf16[3,4,160,256]{3,2,1,0:T(8,128)(2,1)} %get-tuple-element.4) | data formatting | bytes 1966080
  77.4 2.2 %copy.10 = f32[3,3,3,32,256]{4,3,2,1,0:T(8,128)} copy(f32[3,3,3,32,256]{4,3,2,1,0:T(8,128)} %get-tuple-element.5) | data formatting | bytes 1769472

commit v2 on v1

--- a/solution.py
+++ b/solution.py
@@ -39,7 +39,7 @@
 
 def kernel(
     sizes, count_ref, x_ref, g_ref, w_hbm, dx_ref, dw_ref,
-    w_ref, own, prev, nxt, last, shifted, patches, x_t, dx_acc, acc, part, done,
+    w_ref, w_t, own, prev, nxt, last, patches, x_t, dx_acc, acc, part, done,
     a_out, a_in, x_out, x_in, z_out, z_in, fin,
     w_sem, row_send, row_recv, frame_send, frame_recv, rim_send, rim_recv,
     a_send, a_recv, x_send, x_recv, z_send, z_recv, f_send, f_recv,
@@ -119,21 +119,13 @@
         return jnp.concatenate([right, row, left], axis=-1)
 
     def center(frame, row, block):
-        patches[1, frame, row] = spread(block)
+        patches[frame, row + 1] = spread(block)
 
     def rim(frame):
-        top = spread(prev[frame])
-        shifted[...] = spread(nxt[frame])
-        patches[2, frame, 0] = top
+        patches[frame, 0] = spread(prev[frame])
+        patches[frame, rows + 1] = spread(nxt[frame])
         for r in range(1, rows):
-            patches[2, frame, r] = patches[1, frame, r - 1]
-        for r in range(rows - 1):
-            inside = (r + 1 < count).astype(jnp.int32)
-            keep = jnp.broadcast_to(inside, (width, 3 * chans)) > 0
-            patches[0, frame, r] = jnp.where(
-                keep, patches[1, frame, r + 1].astype(F32), shifted[...].astype(F32)
-            ).astype(BF16)
-        patches[0, frame, rows - 1] = shifted[...]
+            patches[frame, r + 1] = patches[frame, jnp.where(r < count, r + 1, rows + 1)]
 
     def frame_inside(f, _):
         for r in range(rows):
@@ -141,6 +133,7 @@
         masked = [
             x_ref[f, r].astype(F32) * (r < count).astype(F32) for r in range(rows)
         ]
+        dx_acc[f] = jnp.zeros((plane, chans), F32)
         x_t[f] = jnp.concatenate(masked, axis=0).T.astype(BF16)
         return 0
 
@@ -186,7 +179,7 @@
         for k in range(3):
             total = None
             for f in range(frames):
-                block = patches[kh, shift + f, :, :, k * chans : (k + 1) * chans]
+                block = patches[shift + f, pl.ds(2 - kh, rows), :, k * chans : (k + 1) * chans]
                 term = jnp.dot(x_t[f], block.reshape(plane, chans), preferred_element_type=F32)
                 total = term if total is None else total + term
             for half in range(2):
@@ -198,21 +191,17 @@
 
     def grad_x(g):
         shift, kh = taps(g)
-        kernel_taps = [w_ref[2 - shift, kh, k] for k in range(3)]
-        wide = jnp.concatenate(kernel_taps, axis=-1)
         for f in range(frames):
-            block = patches[kh, shift + f].reshape(plane, 3 * chans)
-            term = lax.dot_general(
-                block, wide, (((1,), (1,)), ((), ())), preferred_element_type=F32
+            block = patches[shift + f, pl.ds(2 - kh, rows)].reshape(plane, 3 * chans)
+            dx_acc[f] = dx_acc[f] + jnp.dot(
+                block, w_t[2 - shift, kh], preferred_element_type=F32
             )
 
-            @pl.when(g == 0)
-            def _():
-                dx_acc[f] = term
-
-            @pl.when(g > 0)
-            def _():
-                dx_acc[f] = dx_acc[f] + term
+    def turn_w(i, _):
+        kt, kh = i // 3, lax.rem(i, 3)
+        for k in range(3):
+            w_t[kt, kh, k * chans : (k + 1) * chans] = w_ref[kt, kh, k].T
+        return 0
 
     def send_a(g):
         return copy(a_out.at[g], a_in.at[g], a_send.at[g], a_recv.at[g], pair, tile)
@@ -291,26 +280,27 @@
         def _():
             grad_w(s)
 
-        @pl.when(s == GROUPS)
+        @pl.when(s == 0)
         def _():
             load_w.wait()
-
-        @pl.when((s >= GROUPS) & (s < 2 * GROUPS))
-        def _():
-            grad_x(s - GROUPS)
+            lax.fori_loop(0, 9, turn_w, 0)
+
+        @pl.when((s < 3) | ((s >= GROUPS) & (s < GROUPS + 6)))
+        def _():
+            grad_x(s - 6 * (s // GROUPS))
 
         @pl.when((s >= 1) & (s < 1 + GROUPS))
         def _():
             pairs_step(s - 1)
 
-        for start, act in ((8, final_step), (6, z_step), (4, x_step)):
+        for start, act in ((4, x_step), (8, z_step), (12, final_step)):
             @pl.when((s >= start) & (s < start + 2 * GROUPS) & (lax.rem(s, 2) == 0))
             def _():
                 act((s - start) // 2)
 
         return 0
 
-    lax.fori_loop(0, 8 + 2 * GROUPS - 1, step, 0)
+    lax.fori_loop(0, 12 + 2 * GROUPS - 1, step, 0)
 
     for f in range(frames):
         for r in range(rows):
@@ -372,12 +362,12 @@
         out_specs=(pl.BlockSpec(memory_space=vmem), pl.BlockSpec(memory_space=vmem)),
         scratch_shapes=[
             vmem((3, 3, 3, chans, chans), BF16),
+            vmem((3, 3, 3 * chans, chans), BF16),
             vmem((2, rows, width, chans), BF16),
             vmem((full, width, chans), BF16),
             vmem((full, width, chans), BF16),
             vmem((frames, width, chans), BF16),
-            vmem((width, 3 * chans), BF16),
-            vmem((3, full, rows, width, 3 * chans), BF16),
+            vmem((full, rows + 2, width, 3 * chans), BF16),
             vmem((frames, chans, rows * width), BF16),
             vmem((frames, rows * width, chans), F32),
             vmem((GROUPS, 6, nz, nx, slab, LANES), F32),

time: 79.8 us -> 64.3 us (0.81)
  Pallas kernels: 73.9 us -> 58.4 us
    pallas_call x1, Pallas kernels: 73.9 us -> 58.4 us  [body(): pl.pallas_call(functools.partial(kernel, sizes), out_shape=(jax.ShapeDtyp...]
where the time goes in v2:
time: 64.3 us; the launch traced here: 64 us
  Pallas kernels  58.4 us (91%)
  local copies, waits for them, and re-layouts  4.38 us (7%)
  between operations  1.29 us (2%)
    pallas_call x1, Pallas kernels, body(): pl.pallas_call(functools.partial(kernel, sizes), out_shape=(jax.ShapeDtyp...  58.4 us
    unnamed x2, local copies, waits for them, and re-layouts  4.38 us

profile of v2, /device:TPU:0, one launch (start us, length us, event | category | flops | bytes accessed | tf_op | source)
XLA Modules:
  0.0 64.0 jit_solution(12053962926352269088)
XLA Ops:
  1.3 58.4 %shard_map.59 = (bf16[3,4,160,256]{3,2,1,0:T(8,128)(2,1)}, f32[3,3,3,32,256]{4,3,2,1,0:T(8,128)}) custom-call(s32[1]{0:T(128)S(6)} %copy.8.count_ref, bf16[3,4,160,256]{3,2,1,0:T(8,128)(2,1)} %x_ref.1, bf16[3,4,160,256]{3,2,1,0:T(8,128)(2,1)} %g_ref.1, bf16[3,3,3,256,256]{4,3,2,1,0:T(8,128)(2,1)} %w_hbm.1), custom_call_target="tpu_custom_call" | custom-call | flops 13589544960 | bytes 8388608 | tf_op jit(solution)/shard_map/pallas_call | solution.py:350
  59.6 2.2 %copy.9 = bf16[3,4,160,256]{3,2,1,0:T(8,128)(2,1)} copy(bf16[3,4,160,256]{3,2,1,0:T(8,128)(2,1)} %get-tuple-element.4) | data formatting | bytes 1966080
  61.9 2.2 %copy.10 = f32[3,3,3,32,256]{4,3,2,1,0:T(8,128)} copy(f32[3,3,3,32,256]{4,3,2,1,0:T(8,128)} %get-tuple-element.5) | data formatting | bytes 1769472

commit v3 on v2

--- a/solution.py
+++ b/solution.py
@@ -272,35 +272,37 @@
         def _():
             rows_arrive()
 
-        @pl.when(s == 3)
+        @pl.when(s == 5)
         def _():
             frames_arrive()
 
-        @pl.when(s < GROUPS)
-        def _():
-            grad_w(s)
+        @pl.when((s < 3) | ((s >= 5) & (s < 11)))
+        def _():
+            grad_w(s - 2 * ((s + 3) // 8))
 
         @pl.when(s == 0)
         def _():
             load_w.wait()
             lax.fori_loop(0, 9, turn_w, 0)
 
-        @pl.when((s < 3) | ((s >= GROUPS) & (s < GROUPS + 6)))
-        def _():
-            grad_x(s - 6 * (s // GROUPS))
-
-        @pl.when((s >= 1) & (s < 1 + GROUPS))
-        def _():
-            pairs_step(s - 1)
-
-        for start, act in ((4, x_step), (8, z_step), (12, final_step)):
-            @pl.when((s >= start) & (s < start + 2 * GROUPS) & (lax.rem(s, 2) == 0))
+        @pl.when((s < 3) | ((s >= 11) & (s < 17)))
+        def _():
+            grad_x(s - 8 * ((s + 5) // 16))
+
+        for act, early, late, pace in (
+            (pairs_step, 1, 6, 1), (x_step, 2, 8, 2), (z_step, 6, 12, 2), (final_step, 8, 16, 2)
+        ):
+            @pl.when((s >= early) & (s < early + 3))
             def _():
-                act((s - start) // 2)
+                act(s - early)
+
+            @pl.when((s >= late) & (s < late + 6 * pace) & (lax.rem(s - late + 60, pace) == 0))
+            def _():
+                act(3 + (s - late) // pace)
 
         return 0
 
-    lax.fori_loop(0, 12 + 2 * GROUPS - 1, step, 0)
+    lax.fori_loop(0, 27, step, 0)
 
     for f in range(frames):
         for r in range(rows):

time: 64.3 us -> 67.3 us (1.047)
  Pallas kernels: 58.4 us -> 61.4 us
    pallas_call x1, Pallas kernels: 58.4 us -> 61.4 us  [body(): pl.pallas_call(functools.partial(kernel, sizes), out_shape=(jax.ShapeDtyp...]
where the time goes in v3:
time: 67.3 us; the launch traced here: 67.1 us
  Pallas kernels  61.4 us (91%)
  local copies, waits for them, and re-layouts  4.38 us (7%)
  between operations  1.29 us (2%)
    pallas_call x1, Pallas kernels, body(): pl.pallas_call(functools.partial(kernel, sizes), out_shape=(jax.ShapeDtyp...  61.4 us
    unnamed x2, local copies, waits for them, and re-layouts  4.38 us

profile of v3, /device:TPU:0, one launch (start us, length us, event | category | flops | bytes accessed | tf_op | source)
XLA Modules:
  0.0 67.1 jit_solution(13575814962316560054)
XLA Ops:
  1.3 61.4 %shard_map.59 = (bf16[3,4,160,256]{3,2,1,0:T(8,128)(2,1)}, f32[3,3,3,32,256]{4,3,2,1,0:T(8,128)}) custom-call(s32[1]{0:T(128)S(6)} %copy.8.count_ref, bf16[3,4,160,256]{3,2,1,0:T(8,128)(2,1)} %x_ref.1, bf16[3,4,160,256]{3,2,1,0:T(8,128)(2,1)} %g_ref.1, bf16[3,3,3,256,256]{4,3,2,1,0:T(8,128)(2,1)} %w_hbm.1), custom_call_target="tpu_custom_call" | custom-call | flops 13589544960 | bytes 8388608 | tf_op jit(solution)/shard_map/pallas_call | solution.py:352
  62.7 2.2 %copy.9 = bf16[3,4,160,256]{3,2,1,0:T(8,128)(2,1)} copy(bf16[3,4,160,256]{3,2,1,0:T(8,128)(2,1)} %get-tuple-element.4) | data formatting | bytes 1966080
  64.9 2.2 %copy.10 = f32[3,3,3,32,256]{4,3,2,1,0:T(8,128)} copy(f32[3,3,3,32,256]{4,3,2,1,0:T(8,128)} %get-tuple-element.5) | data formatting | bytes 1769472
